TPU v7x, 256 devices: a whole 4x4x8 slice. The times are simulated.
256 devices in a mesh: pb: 8 (over z_lo, y), ka: 32 (over z_hi, x, core).
Axes of the slice: x: 4, y: 4, z: 8 (z_hi: 4, z_lo: 2; z = z_hi * 2 + z_lo), core: 2. Of those that a mesh axis runs over, the one named last changes fastest.
Arguments:
- query_features: bfloat16 [32768, 128], P(('pb', 'ka')), may hold values from -240 to 240, as said below
- key_features: bfloat16 [131072, 128], P(('ka', 'pb')), may hold values from -16 to 16, as said below
Outputs:
- forward_flow: float32 [2, 32768], P(None, ('pb', 'ka'))
- backward_flow: float32 [2, 131072], P(None, ('ka', 'pb'))
Inputs may be any that keep to these rules, and one draw needn't show every extreme that they name: `query_features`: finite feature values. `key_features`: finite feature values.
All inputs are finite; a program needn't handle non-finite values.
Results may differ from a plain program's by a relative error of at most 0.0009.
Values may be sent and summed in bfloat16 or wider, within the bound.
No kernel may reach another device: no remote copies, remote signals or barrier semaphores. Data moves between devices by JAX's collectives and lax.ppermute only.
A program may use at most 192 MiB of HBM per device.

v0:
```python
import functools
import math

import jax
import jax.numpy as jnp
from jax import lax
from jax.experimental import pallas as pl
from jax.experimental.pallas import tpu as pltpu
from jax.sharding import Mesh
from jax.sharding import PartitionSpec as P

FRAME_W = 480
CH = 128
BAND = 4096
PIECE = 512
RUN = 32
TILES = 4
UNROLL = 8
SCALE = math.log2(math.e) / math.sqrt(CH)
LOW, HIGH = 2.0**-90, 2.0**100
AXES = ("zl", "y", "zh", "x", "core")
SIZES = {"zl": 2, "y": 4, "zh": 4, "x": 4, "core": 2}
NT = (((1,), (1,)), ((), ()))
CORE, X, Y, Z, PIECE_Z = 0, 1, 2, 3, 4


def nt_dot(a, b):
    return lax.dot_general(a, b, NT, preferred_element_type=jnp.float32)


def split2(v):
    high = v.astype(jnp.bfloat16)
    return high, (v - high.astype(jnp.float32)).astype(jnp.bfloat16)


def cell(n):
    y = ((n >> 5) * 4370) >> 16
    return (n - y * FRAME_W).astype(jnp.float32), y.astype(jnp.float32)


def iota(shape, axis):
    return lax.broadcasted_iota(jnp.int32, shape, axis)


def key_base(z, y, x, core):
    return ((((z >> 1) * 4 + x) * 2 + core) * 8 + (z & 1) * 4 + y) * 512


def query_base(z, y, x, core):
    return ((((z & 1) * 4 + y) * 4 + (z >> 1)) * 8 + x * 2 + core) * 128


def key_weights(sc):
    lane = iota((16, 256), 1)
    row = iota((16, 256), 0)
    on_sum = lane < 128
    s, g = (lane >> 4) & 7, lane & 15
    x, y = cell(key_base(sc[Z], sc[Y], s & 3, s >> 2) + g * RUN)
    x, y = x + (RUN - 256.0), y - 128.0
    value = jnp.where(row == 0, 1.0, jnp.where(row == 1, x, jnp.where(row == 2, y, 0.0)))
    value = jnp.where(on_sum, value, jnp.where(row == 1, -1.0, 0.0))
    return value.astype(jnp.bfloat16)


def query_weights(sc, z, half):
    r = iota((8, 128), 0)
    slot = jnp.where(r < 4, 2 * half, 2 * half + 1)
    x, y = cell(query_base(z, sc[Y] ^ slot, sc[X], sc[CORE]) + (r & 3) * RUN)
    return x + (RUN - 256.0), y


def run_order():
    r, c = iota((256, 256), 0), iota((256, 256), 1)
    return jnp.where(c == (r & 7) * RUN + (r >> 3), 1.0, 0.0).astype(jnp.bfloat16)


def set_keys(sc, ka, kb, kp):
    perm = run_order()
    for core, ref in ((sc[CORE], ka), (1 - sc[CORE], kb)):
        for j in range(4):
            shard = core * 4 + (sc[X] ^ j)
            low, high = (
                jnp.dot(perm, ref[at : at + 256, :], preferred_element_type=jnp.float32)
                for at in (j * 512, j * 512 + 256)
            )
            for t in range(RUN):
                rows = jnp.concatenate([low[t * 8 : t * 8 + 8], high[t * 8 : t * 8 + 8]], 0)
                at = pl.multiple_of(t * 128 + shard * 16, 16)
                kp[pl.ds(at, 16), :] = rows.astype(jnp.bfloat16)


def set_queries(refs, qp, plain=False):
    perm = run_order()
    for i, ref in enumerate(refs):
        for half in range(2):
            rows = slice(half * 256, half * 256 + 256)
            got = jnp.dot(perm, ref[rows, :], preferred_element_type=jnp.float32)
            to = slice(i * PIECE + half * 256, i * PIECE + half * 256 + 256)
            if plain:
                qp[to, :] = got.astype(jnp.bfloat16)
            else:
                qp[to, 0:CH], qp[to, CH : 2 * CH] = split2(got * SCALE)


def in_order(refs, part):
    got = []
    for run in range(4 * part, 4 * part + 4):
        there = pl.ds((run // 8) * 256 + run % 8, RUN, stride=8)
        got.append(jnp.concatenate([ref[there, :] for ref in refs], 1))
    return split2(jnp.concatenate(got, 0))


def block(sc, zs, qp, kp, acc, sums_ref, moments_ref, store, tops=None):
    tiles = TILES if tops is None else 1
    halves = 2 * len(zs)
    sums_ref[...] = jnp.zeros_like(sums_ref)
    moments_ref[...] = jnp.zeros_like(moments_ref)
    weights = [query_weights(sc, zs[half // 2], half % 2) for half in range(halves)]

    def chunk(j, carry):
        at = pl.multiple_of(j * tiles * 128, tiles * 128)
        lanes = pl.ds(at, tiles * 128)
        if tops is None:
            keys = kp[lanes, :]
            s = nt_dot(qp[0 : halves * 256, :], jnp.concatenate([keys, keys], 1))
            for_query = for_key = jnp.exp2(s)
        else:
            s = nt_dot(qp[...], kp[lanes, :]) * SCALE
            for_query = jnp.exp2(s - tops[0][...])
            for_key = jnp.exp2(s - tops[1][0:1, lanes])
        for half in range(halves):
            sums, moments = [None] * tiles, [None] * tiles
            for u in range(RUN):
                rows = slice(half * 256 + u * 8, half * 256 + u * 8 + 8)
                own_sum, own_moment = sums_ref[rows, :], moments_ref[rows, :]
                for i in range(tiles):
                    part = (rows, slice(i * 128, i * 128 + 128))
                    e = for_key[part]
                    sums[i] = e if u == 0 else sums[i] + e
                    moments[i] = sums[i] if u == 0 else moments[i] + sums[i]
                    own_sum = own_sum + for_query[part]
                    own_moment = own_moment + own_sum
                sums_ref[rows, :] = own_sum
                moments_ref[rows, :] = own_moment
            x, y = weights[half]
            for i in range(tiles):
                d = pl.ds(pl.multiple_of(at + i * 128, 128), 128)
                acc[0, :, d] += sums[i]
                acc[1, :, d] += sums[i] * x - moments[i]
                acc[2, :, d] += sums[i] * y
        return carry

    lax.fori_loop(0, BAND // 128 // tiles, chunk, 0, unroll=UNROLL if tops is None else 1)
    w = key_weights(sc)
    for piece in range(len(zs)):
        for slot in range(4):
            hi, lo = in_order((sums_ref, moments_ref), 4 * piece + slot)
            store(piece, slot, slice(0, 3), (nt_dot(w, hi) + nt_dot(w, lo))[0:3])


def spread_keys(sc, near, far, spread, acc, top=None):
    lane = iota((8, 128), 1) >> 4
    for stat in range(4):
        if stat == 3 and top is None:
            near[:, 3:4, :] = jnp.zeros((4, 1, 512), jnp.float32)
            far[:, 3:4, :] = jnp.zeros((4, 1, 512), jnp.float32)
            continue
        for part in range(4):
            out = jnp.zeros((8, 128), jnp.float32)
            for t in range(8):
                d = slice((part * 8 + t) * 128, (part * 8 + t) * 128 + 128)
                value = top[0:1, d] if stat == 3 else jnp.sum(acc[stat, :, d], 0, keepdims=True)
                value = pltpu.roll(jnp.broadcast_to(value, (8, 128)), 0, 1, stride=16, stride_axis=0)
                out = jnp.where(lane == t, pltpu.roll(value, (t * 16 + 16) % 128, 1), out)
            spread[:, part * 128 : part * 128 + 128] = out
        for i, ref in enumerate((near, far)):
            for j in range(4):
                row = 7 - ((sc[CORE] ^ i) * 4 + (sc[X] ^ j))
                ref[j, stat : stat + 1, :] = spread[pl.ds(row, 1), :]


def first_kernel(sc, ka, kb, q, kp, acc, rows, qp, sums_ref, moments_ref):
    set_keys(sc, ka, kb, kp)
    acc[...] = jnp.zeros_like(acc)
    set_queries([q], qp)

    def store(piece, slot, stats, value):
        rows[piece, slot, stats, :] = value

    block(sc, [sc[PIECE_Z]], qp, kp, acc, sums_ref, moments_ref, store)


def more_kernel(first, sc, kp, old, *refs):
    count = len(refs) - 5
    qs, (acc, rows, qp, sums_ref, moments_ref) = refs[:count], refs[count:]
    acc[...] = old[...]
    set_queries(qs, qp)

    def store(piece, slot, stats, value):
        rows[piece, slot, stats, :] = value

    zs = [sc[PIECE_Z + first + i] for i in range(count)]
    block(sc, zs, qp, kp, acc, sums_ref, moments_ref, store)


def last_kernel(sc, kp, old, q, r0, r1, r2, r3, *refs):
    pieces, refs = refs[:8], refs[8:]
    row_ref, near, far, acc, qp, sums_ref, moments_ref, spread, rm, km, raw, qx, sem = refs
    acc[...] = old[...]
    set_queries([q], qp)

    def place(piece, slot):
        return sc[PIECE_Z + piece] * 4 + (sc[Y] ^ slot)

    def store(piece, slot, stats, value):
        row_ref[place(piece, slot), stats, :] = value

    block(
        sc, [sc[PIECE_Z + 7]], qp, kp, acc, sums_ref, moments_ref,
        lambda _, *what: store(7, *what),
    )
    piece = 0
    for ref in (r0, r1, r2, r3):
        for i in range(ref.shape[0]):
            for slot in range(4):
                store(piece, slot, slice(0, 3), ref[i, slot, 0:3, :])
            piece += 1
    row_ref[:, 3:4, :] = jnp.zeros((32, 1, 128), jnp.float32)
    spread_keys(sc, near, far, spread, acc)
    sums = [row_ref[:, 0, :], near[:, 0, :], far[:, 0, :]]
    low = functools.reduce(jnp.minimum, [jnp.min(v) for v in sums])
    high = functools.reduce(jnp.maximum, [jnp.max(v) for v in sums])

    @pl.when(jnp.logical_not((low > LOW) & (high < HIGH)))
    def _():
        acc[...] = jnp.zeros_like(acc)
        km[...] = jnp.full_like(km, -jnp.inf)
        pick = jnp.where((iota((16, 128), 0) == 0) & (iota((16, 128), 1) == 0), 1.0, 0.0)
        pick = pick.astype(jnp.bfloat16)

        def fetch(piece):
            copy = pltpu.make_async_copy(pieces[piece], raw, sem)
            copy.start()
            copy.wait()
            set_queries([raw], qx, True)

        def block_top(half, t):
            lanes = pl.ds(pl.multiple_of(t * 128, 128), 128)
            s = nt_dot(qx[half * 256 : half * 256 + 256, :], kp[lanes, :]) * SCALE
            return lanes, s

        for piece in range(8):
            fetch(piece)

            def chunk(t, carry):
                for half in range(2):
                    lanes, s = block_top(half, t)
                    km[:, lanes] = jnp.maximum(km[:, lanes], jnp.max(s.reshape(RUN, 8, 128), 0))
                return carry

            lax.fori_loop(0, BAND // 128, chunk, 0)
        km[...] = jnp.broadcast_to(jnp.max(km[...], 0, keepdims=True), km.shape)
        for piece in range(8):
            fetch(piece)
            for half in range(2):

                def chunk(t, top, half=half):
                    return jnp.maximum(top, block_top(half, t)[1])

                top = jnp.full((256, 128), -jnp.inf, jnp.float32)
                top = lax.fori_loop(0, BAND // 128, chunk, top)
                hi, lo = split2(jnp.broadcast_to(jnp.max(top, 1, keepdims=True), (256, 128)))
                rm[half * 256 : half * 256 + 256, :] = hi.astype(jnp.float32) + lo.astype(
                    jnp.float32
                )
            for slot in range(4):
                hi, lo = in_order((rm,), slot)
                store(piece, slot, slice(3, 4), (nt_dot(pick, hi) + nt_dot(pick, lo))[0:1])
            block(
                sc, [sc[PIECE_Z + piece]], qx, kp, acc, sums_ref, moments_ref,
                lambda _, *what, piece=piece: store(piece, *what), (rm, km),
            )
        spread_keys(sc, near, far, spread, acc, km)


def merged(parts):
    top = parts[0][3:4]
    for part in parts[1:]:
        top = jnp.maximum(top, part[3:4])
    return sum(part[0:3] * jnp.exp2(part[3:4] - top) for part in parts), top


def merge_kernel(a, b, *outs):
    r, c = iota((512, 512), 0), iota((512, 512), 1)
    order = jnp.where(c == (r & 15) * RUN + (r >> 4), 1.0, 0.0).astype(jnp.bfloat16)
    rows = []
    for j in range(4):
        rows += list(merged([a[j], b[j]]))
    left = jnp.concatenate(rows, 0)
    parts = []
    for _ in range(3):
        parts.append(left.astype(jnp.bfloat16))
        left = left - parts[-1].astype(jnp.float32)
    got = jnp.dot(jnp.concatenate(parts, 0), order, preferred_element_type=jnp.float32)
    got = got[0:16] + got[16:32] + got[32:48]
    for j, out in enumerate(outs):
        out[...] = got[4 * j : 4 * j + 4]


def final_kernel(sc, rows, k0, k1, k2, k3, f_ref, b_ref):
    top = rows[:, 3, :]
    w = jnp.exp2(top - jnp.max(top, 0, keepdims=True))
    q = [jnp.sum(rows[:, stat, :] * w, 0, keepdims=True) for stat in range(3)]
    x, y = cell(query_base(sc[Z], sc[Y], sc[X], sc[CORE]) + iota((1, 128), 1))
    f_ref[0:1, :] = (q[1] / q[0] + (256.0 - x)) / FRAME_W
    f_ref[1:2, :] = (q[2] / q[0] + (128.0 - y)) / FRAME_W
    k, _ = merged([ref[...] for ref in (k0, k1, k2, k3)])
    x, y = cell(key_base(sc[Z], sc[Y], sc[X], sc[CORE]) + iota((1, 512), 1))
    b_ref[0:1, :] = (k[1:2] / k[0:1] + (256.0 - x)) / FRAME_W
    b_ref[1:2, :] = (k[2:3] / k[0:1] - y) / FRAME_W


def coords(i):
    out = {}
    for name in reversed(AXES):
        out[name] = i % SIZES[name]
        i //= SIZES[name]
    return out


def index(at):
    return functools.reduce(lambda a, name: a * SIZES[name] + at[name], AXES, 0)


def swap(value, **flips):
    def partner(i):
        at = coords(i)
        for name, flip in flips.items():
            at[name] ^= flip
        return index(at)

    return lax.ppermute(value, AXES, [(i, partner(i)) for i in range(256)])


def ring(value, odd):
    def partner(i):
        at = coords(i)
        z = (((at["zh"] * 2 + at["zl"] + odd) ^ 1) - odd) % 8
        at["zh"], at["zl"] = z // 2, z % 2
        return index(at)

    return lax.ppermute(value, AXES, [(i, partner(i)) for i in range(256)])


SMEM = pl.BlockSpec(memory_space=pltpu.SMEM)
VMEM = pl.BlockSpec(memory_space=pltpu.VMEM)
ANY = pl.BlockSpec(memory_space=pl.ANY)


def f32(*shape):
    return jax.ShapeDtypeStruct(shape, jnp.float32)


def call(kernel, name, args, in_specs, out_shape, scratch, pieces, alias=None):
    return pl.pallas_call(
        kernel,
        name=name,
        out_shape=out_shape,
        in_specs=in_specs,
        out_specs=[VMEM] * len(out_shape),
        scratch_shapes=scratch,
        input_output_aliases=alias or {},
        cost_estimate=pl.CostEstimate(
            flops=pieces * 2 * PIECE * BAND * 256, bytes_accessed=2**21, transcendentals=pieces * PIECE * BAND
        ),
        compiler_params=pltpu.CompilerParams(vmem_limit_bytes=40 * 2**20),
    )(*args)


def on_device(q, k):
    me = {name: lax.axis_index(name) for name in AXES}
    z = me["zh"] * 2 + me["zl"]
    by_y = [swap(q, y=j) for j in (1, 3, 2)]
    by_x = [swap(k, x=j) for j in (1, 3, 2)]
    by_y, by_x = lax.optimization_barrier((by_y, by_x))
    own = jnp.concatenate([q, by_y[0], by_y[2], by_y[1]])
    ka = jnp.concatenate([k, by_x[0], by_x[2], by_x[1]])
    kb = swap(ka, core=1)
    ahead = 1 - 2 * (z & 1)
    z_of = [(z + off * ahead) % 8 for off in (0, 1, -1, 2, -2, 3, -3, 4)]
    sc = jnp.stack([me["core"], me["x"], me["y"], z] + z_of).astype(jnp.int32)

    half_sums = [pltpu.VMEM((PIECE, 128), jnp.float32)] * 2
    piece_rows = pltpu.VMEM((PIECE, 2 * CH), jnp.bfloat16)
    plain = [pltpu.VMEM((PIECE, CH), jnp.bfloat16)] * 2
    two = [pltpu.VMEM((2 * PIECE, 2 * CH), jnp.bfloat16)] + [pltpu.VMEM((2 * PIECE, 128), jnp.float32)] * 2
    pieces = [own, ring(own, 0), ring(own, 1)]
    kp, acc, r0 = call(
        first_kernel, "first", (sc, ka, kb, own), [SMEM, VMEM, VMEM, VMEM],
        [jax.ShapeDtypeStruct((BAND, CH), jnp.bfloat16), f32(3, 8, BAND), f32(1, 4, 4, 128)],
        [piece_rows] + half_sums, 1,
    )
    parts = [r0]
    for first in (1, 3, 5):
        up, down, acc = lax.optimization_barrier((pieces[first], pieces[first + 1], acc))
        pieces += [ring(down, 0), ring(up, 1)] if first < 5 else [ring(down, 0)]
        acc, got = call(
            functools.partial(more_kernel, first), f"more{first}",
            (sc, kp, acc, up, down), [SMEM] + [VMEM] * 4,
            [f32(3, 8, BAND), f32(2, 4, 4, 128)], two, 2,
        )
        parts.append(got)
    rows, near, far = call(
        last_kernel, "last", (sc, kp, acc, pieces[7], *parts, *pieces),
        [SMEM] + [VMEM] * 7 + [ANY] * 8, [f32(32, 4, 128), f32(4, 4, 512), f32(4, 4, 512)],
        [pltpu.VMEM((3, 8, BAND), jnp.float32), piece_rows] + half_sums
        + [pltpu.VMEM((8, 512), jnp.float32), pltpu.VMEM((PIECE, 128), jnp.float32),
           pltpu.VMEM((8, BAND), jnp.float32), *plain, pltpu.SemaphoreType.DMA], 1,
    )
    cols = call(
        merge_kernel, "merge", (near, swap(far, core=1)), [VMEM] * 2, [f32(4, 512)] * 4, [], 0
    )
    cols = [cols[0]] + [swap(cols[j], x=j) for j in (1, 3, 2)]
    rows = lax.all_to_all(rows, ("zh", "zl", "y"), 0, 0)
    return call(
        final_kernel, "finish", (sc, rows, *cols), [SMEM] + [VMEM] * 5, [f32(2, 128), f32(2, 512)], [], 0
    )


def solution(mesh):
    fine = Mesh(mesh.devices.reshape(tuple(SIZES[name] for name in AXES)), AXES)
    key = ("zh", "x", "core", "zl", "y")
    return jax.shard_map(
        on_device,
        mesh=fine,
        in_specs=(P(AXES), P(key)),
        out_specs=(P(None, AXES), P(None, key)),
        check_vma=False,
    )
```

profile of v0, /device:TPU:1, one launch (start us, length us, event | category | flops | bytes accessed | tf_op | source)
XLA Modules:
  0.0 285.1 jit_solution(11585602110635944961)
XLA Ops:
  0.6 2.2 collective-permute-start
  2.8 1.2 collective-permute-start.3
  4.1 1.8 collective-permute-start.4
  6.5 1.9 collective-permute-start.1
  9.1 0.9 constant_dynamic-update-slice_fusion.3
  10.1 0.9 collective-permute-done.1
  11.0 2.2 collective-permute-done.2
  13.3 2.7 collective-permute-start.6
  16.1 1.7 collective-permute-start.7
  17.8 4.7 %collective-permute-start.8 = (bf16[512,128]{1,0:T(8,128)(2,1)S(1)}, bf16[512,128]{1,0:T(8,128)(2,1)S(1)}, u32[]{:S(2)}, u32[]{:S(2)}) collective-permute-start(bf16[512,128]{1,0:T(8,128)(2,1)S(1)} %constant_dynamic-update-slice_fusion.4.q.refs_0_), channel_id=1, source_target_pairs={{0,152},{1,153},{2,154},{3,155},{4,156},{5,157},{6,158},{7,159},{8... | collective-permute-start | bytes 393224 | tf_op jit(solution)/shard_map/ppermute | solution.py:352
  22.6 3.4 %first.1 = (bf16[4096,128]{1,0:T(8,128)(2,1)S(1)}, f32[3,8,4096]{2,1,0:T(8,128)S(1)}, f32[1,4,4,128]{3,2,1,0:T(4,128)S(1)}) custom-call(s32[12]{0:T(128)S(1)} %stack.51.sc, bf16[2048,128]{1,0:T(8,128)(2,1)S(1)} %constant_dynamic-update-slice_fusion.ka, bf16[2048,128]{1,0:T(8,128)(2,1)S(1)} %collective-permute-done.6.kb, ...), custom_call_target="tpu_custom_call" | custom-call | flops 1073741824 | bytes 2097152 | tf_op jit(solution)/shard_map/first/pallas_call | solution.py:365
  26.0 1.5 collective-permute-start.10
  27.5 4.9 %more1.1 = (f32[3,8,4096]{2,1,0:T(8,128)S(1)}, f32[2,4,4,128]{3,2,1,0:T(4,128)S(1)}) custom-call(s32[12]{0:T(128)S(1)} %stack.51.sc, bf16[4096,128]{1,0:T(8,128)(2,1)S(1)} %get-tuple-element.39.kp, f32[3,8,4096]{2,1,0:T(8,128)S(1)} %get-tuple-element.43.old, bf16[512,128]{1,0:T(8,128)(2,1)S(1)} %collective-permute-done.7.refs_0_.refs_1_, ...), custom_call_target="tpu_custom_call" | custom-call | flops 2147483648 | bytes 2097152 | tf_op jit(solution)/shard_map/more1/pallas_call | solution.py:365
  32.4 1.6 collective-permute-start.11
  33.9 1.2 collective-permute-start.12
  35.2 4.9 %more3.1 = (f32[3,8,4096]{2,1,0:T(8,128)S(1)}, f32[2,4,4,128]{3,2,1,0:T(4,128)S(1)}) custom-call(s32[12]{0:T(128)S(1)} %stack.51.sc, bf16[4096,128]{1,0:T(8,128)(2,1)S(1)} %get-tuple-element.39.kp, f32[3,8,4096]{2,1,0:T(8,128)S(1)} %get-tuple-element.47.old, bf16[512,128]{1,0:T(8,128)(2,1)S(1)} %collective-permute-done.9.refs_0_.refs_3_, ...), custom_call_target="tpu_custom_call" | custom-call | flops 2147483648 | bytes 2097152 | tf_op jit(solution)/shard_map/more3/pallas_call | solution.py:365
  40.4 4.9 %more5.1 = (f32[3,8,4096]{2,1,0:T(8,128)S(1)}, f32[2,4,4,128]{3,2,1,0:T(4,128)S(1)}) custom-call(s32[12]{0:T(128)S(1)} %stack.51.sc, bf16[4096,128]{1,0:T(8,128)(2,1)S(1)} %get-tuple-element.39.kp, f32[3,8,4096]{2,1,0:T(8,128)S(1)} %get-tuple-element.49.old, bf16[512,128]{1,0:T(8,128)(2,1)S(1)} %collective-permute-done.11.refs_0_.refs_5_, ...), custom_call_target="tpu_custom_call" | custom-call | flops 2147483648 | bytes 2097152 | tf_op jit(solution)/shard_map/more5/pallas_call | solution.py:365
  45.3 221.3 %last.1 = (f32[32,4,128]{2,1,0:T(4,128)}, f32[4,4,512]{2,1,0:T(4,128)S(1)}, f32[4,4,512]{2,1,0:T(4,128)S(1)}) custom-call(s32[12]{0:T(128)S(1)} %stack.51.sc, bf16[4096,128]{1,0:T(8,128)(2,1)S(1)} %get-tuple-element.39.kp, f32[3,8,4096]{2,1,0:T(8,128)S(1)} %get-tuple-element.52.old, bf16[512,128]{1,0:T(8,128)(2,1)S(1)} %collective-permute-done.13.q.refs_7_, ...), custom_call_target="tpu_custom_call" | custom-call | flops 1073741824 | bytes 2097152 | tf_op jit(solution)/shard_map/last/pallas_call | solution.py:365
  266.5 5.7 %all-to-all-start = ((f32[32,4,128]{2,1,0:T(4,128)}), f32[32,4,128]{2,1,0:T(4,128)S(1)}, u32[]{:S(2)}, u32[]{:S(2)}) async-start(f32[32,4,128]{2,1,0:T(4,128)} %get-tuple-element.57), calls=%async_computation | async-start | bytes 131072 | tf_op jit(solution)/shard_map/all_to_all | solution.py:424
  272.2 3.9 %collective-permute-start.14 = (f32[4,4,512]{2,1,0:T(4,128)S(1)}, f32[4,4,512]{2,1,0:T(4,128)S(1)}, u32[]{:S(2)}, u32[]{:S(2)}) collective-permute-start(f32[4,4,512]{2,1,0:T(4,128)S(1)} %get-tuple-element.59), channel_id=1, source_target_pairs={{0,1},{1,0},{2,3},{3,2},{4,5},{5,4},{6,7},{7,6},{8,9},{9,8},{10,11... | collective-permute-start | bytes 98312 | tf_op jit(solution)/shard_map/ppermute | solution.py:342
  277.8 1.8 collective-permute-start.16
  280.4 1.3 collective-permute-done.16.k2
  281.8 2.1 collective-permute-done.17.k3
  283.9 1.2 finish.1
  (32 shorter events, 4.4 us)
Async XLA Ops:
  0.6 7.8 %collective-permute-start = (bf16[128,128]{1,0:T(8,128)(2,1)}, bf16[128,128]{1,0:T(8,128)(2,1)S(1)}, u32[]{:S(2)}, u32[]{:S(2)}) collective-permute-start(bf16[128,128]{1,0:T(8,128)(2,1)} %param.2), channel_id=1, source_target_pairs={{0,32},{1,33},{2,34},{3,35},{4,36},{5,37},{6,38},{7,39},{8,40},{9,... | collective-permute-start | bytes 98312 | tf_op jit(solution)/shard_map/ppermute | solution.py:342
  2.8 10.3 %collective-permute-start.3 = (bf16[512,128]{1,0:T(8,128)(2,1)}, bf16[512,128]{1,0:T(8,128)(2,1)S(1)}, u32[]{:S(2)}, u32[]{:S(2)}) collective-permute-start(bf16[512,128]{1,0:T(8,128)(2,1)} %param.3), channel_id=1, source_target_pairs={{0,2},{1,3},{2,0},{3,1},{4,6},{5,7},{6,4},{7,5},{8,10},{9,11},{10,... | collective-permute-start | bytes 393224 | tf_op jit(solution)/shard_map/ppermute | solution.py:342
  4.1 9.1 %collective-permute-start.4 = (bf16[512,128]{1,0:T(8,128)(2,1)}, bf16[512,128]{1,0:T(8,128)(2,1)S(1)}, u32[]{:S(2)}, u32[]{:S(2)}) collective-permute-start(bf16[512,128]{1,0:T(8,128)(2,1)} %param.3), channel_id=1, source_target_pairs={{0,6},{1,7},{2,4},{3,5},{4,2},{5,3},{6,0},{7,1},{8,14},{9,15},{10,... | collective-permute-start | bytes 393224 | tf_op jit(solution)/shard_map/ppermute | solution.py:342
  5.9 7.3 %collective-permute-start.5 = (bf16[512,128]{1,0:T(8,128)(2,1)}, bf16[512,128]{1,0:T(8,128)(2,1)S(1)}, u32[]{:S(2)}, u32[]{:S(2)}) collective-permute-start(bf16[512,128]{1,0:T(8,128)(2,1)} %param.3), channel_id=1, source_target_pairs={{0,4},{1,5},{2,6},{3,7},{4,0},{5,1},{6,2},{7,3},{8,12},{9,13},{10,... | collective-permute-start | bytes 393224 | tf_op jit(solution)/shard_map/ppermute | solution.py:342
  6.5 4.5 %collective-permute-start.1 = (bf16[128,128]{1,0:T(8,128)(2,1)}, bf16[128,128]{1,0:T(8,128)(2,1)S(1)}, u32[]{:S(2)}, u32[]{:S(2)}) collective-permute-start(bf16[128,128]{1,0:T(8,128)(2,1)} %param.2), channel_id=1, source_target_pairs={{0,96},{1,97},{2,98},{3,99},{4,100},{5,101},{6,102},{7,103},{8,104... | collective-permute-start | bytes 98312 | tf_op jit(solution)/shard_map/ppermute | solution.py:342
  8.4 4.8 %collective-permute-start.2 = (bf16[128,128]{1,0:T(8,128)(2,1)}, bf16[128,128]{1,0:T(8,128)(2,1)S(1)}, u32[]{:S(2)}, u32[]{:S(2)}) collective-permute-start(bf16[128,128]{1,0:T(8,128)(2,1)} %param.2), channel_id=1, source_target_pairs={{0,64},{1,65},{2,66},{3,67},{4,68},{5,69},{6,70},{7,71},{8,72},{9,... | collective-permute-start | bytes 98312 | tf_op jit(solution)/shard_map/ppermute | solution.py:342
  13.3 2.8 copy-start
  13.3 9.3 %collective-permute-start.6 = (bf16[2048,128]{1,0:T(8,128)(2,1)S(1)}, bf16[2048,128]{1,0:T(8,128)(2,1)S(1)}, u32[]{:S(2)}, u32[]{:S(2)}) collective-permute-start(bf16[2048,128]{1,0:T(8,128)(2,1)S(1)} %constant_dynamic-update-slice_fusion.ka), channel_id=1, source_target_pairs={{0,1},{1,0},{2,3},{3,2},{4,5},{5,4},{6,7},{7,6},{8,9},{9,8},{10,11... | collective-permute-start | bytes 1572872 | tf_op jit(solution)/shard_map/ppermute | solution.py:342
  16.1 9.9 %collective-permute-start.7 = (bf16[512,128]{1,0:T(8,128)(2,1)S(1)}, bf16[512,128]{1,0:T(8,128)(2,1)S(1)}, u32[]{:S(2)}, u32[]{:S(2)}) collective-permute-start(bf16[512,128]{1,0:T(8,128)(2,1)S(1)} %constant_dynamic-update-slice_fusion.4.q.refs_0_), channel_id=1, source_target_pairs={{0,128},{1,129},{2,130},{3,131},{4,132},{5,133},{6,134},{7,135},{8... | collective-permute-start | bytes 393224 | tf_op jit(solution)/shard_map/ppermute | solution.py:352
  17.8 8.2 %collective-permute-start.8 = (bf16[512,128]{1,0:T(8,128)(2,1)S(1)}, bf16[512,128]{1,0:T(8,128)(2,1)S(1)}, u32[]{:S(2)}, u32[]{:S(2)}) collective-permute-start(bf16[512,128]{1,0:T(8,128)(2,1)S(1)} %constant_dynamic-update-slice_fusion.4.q.refs_0_), channel_id=1, source_target_pairs={{0,152},{1,153},{2,154},{3,155},{4,156},{5,157},{6,158},{7,159},{8... | collective-permute-start | bytes 393224 | tf_op jit(solution)/shard_map/ppermute | solution.py:352
  26.0 6.4 %collective-permute-start.10 = (bf16[512,128]{1,0:T(8,128)(2,1)S(1)}, bf16[512,128]{1,0:T(8,128)(2,1)S(1)}, u32[]{:S(2)}, u32[]{:S(2)}) collective-permute-start(bf16[512,128]{1,0:T(8,128)(2,1)S(1)} %collective-permute-done.7.refs_0_.refs_1_), channel_id=1, source_target_pairs={{0,152},{1,153},{2,154},{3,155},{4,156},{5,157},{6,158},{7,159},{8... | collective-permute-start | bytes 393224 | tf_op jit(solution)/shard_map/ppermute | solution.py:352
  27.5 4.9 %collective-permute-start.9 = (bf16[512,128]{1,0:T(8,128)(2,1)S(1)}, bf16[512,128]{1,0:T(8,128)(2,1)S(1)}, u32[]{:S(2)}, u32[]{:S(2)}) collective-permute-start(bf16[512,128]{1,0:T(8,128)(2,1)S(1)} %collective-permute-done.8.refs_1_.refs_2_), channel_id=1, source_target_pairs={{0,128},{1,129},{2,130},{3,131},{4,132},{5,133},{6,134},{7,135},{8... | collective-permute-start | bytes 393224 | tf_op jit(solution)/shard_map/ppermute | solution.py:352
  32.4 7.7 %collective-permute-start.11 = (bf16[512,128]{1,0:T(8,128)(2,1)S(1)}, bf16[512,128]{1,0:T(8,128)(2,1)S(1)}, u32[]{:S(2)}, u32[]{:S(2)}) collective-permute-start(bf16[512,128]{1,0:T(8,128)(2,1)S(1)} %collective-permute-done.10.refs_1_.refs_4_), channel_id=1, source_target_pairs={{0,128},{1,129},{2,130},{3,131},{4,132},{5,133},{6,134},{7,135},{8... | collective-permute-start | bytes 393224 | tf_op jit(solution)/shard_map/ppermute | solution.py:352
  33.9 6.1 %collective-permute-start.12 = (bf16[512,128]{1,0:T(8,128)(2,1)S(1)}, bf16[512,128]{1,0:T(8,128)(2,1)S(1)}, u32[]{:S(2)}, u32[]{:S(2)}) collective-permute-start(bf16[512,128]{1,0:T(8,128)(2,1)S(1)} %collective-permute-done.9.refs_0_.refs_3_), channel_id=1, source_target_pairs={{0,152},{1,153},{2,154},{3,155},{4,156},{5,157},{6,158},{7,159},{8... | collective-permute-start | bytes 393224 | tf_op jit(solution)/shard_map/ppermute | solution.py:352
  40.1 5.2 %collective-permute-start.13 = (bf16[512,128]{1,0:T(8,128)(2,1)S(1)}, bf16[512,128]{1,0:T(8,128)(2,1)S(1)}, u32[]{:S(2)}, u32[]{:S(2)}) collective-permute-start(bf16[512,128]{1,0:T(8,128)(2,1)S(1)} %collective-permute-done.12.refs_1_.refs_6_), channel_id=1, source_target_pairs={{0,128},{1,129},{2,130},{3,131},{4,132},{5,133},{6,134},{7,135},{8... | collective-permute-start | bytes 393224 | tf_op jit(solution)/shard_map/ppermute | solution.py:352
  266.5 17.4 %all-to-all-start = ((f32[32,4,128]{2,1,0:T(4,128)}), f32[32,4,128]{2,1,0:T(4,128)S(1)}, u32[]{:S(2)}, u32[]{:S(2)}) async-start(f32[32,4,128]{2,1,0:T(4,128)} %get-tuple-element.57), calls=%async_computation | async-start | bytes 131072 | tf_op jit(solution)/shard_map/all_to_all | solution.py:424
  272.2 4.7 %collective-permute-start.14 = (f32[4,4,512]{2,1,0:T(4,128)S(1)}, f32[4,4,512]{2,1,0:T(4,128)S(1)}, u32[]{:S(2)}, u32[]{:S(2)}) collective-permute-start(f32[4,4,512]{2,1,0:T(4,128)S(1)} %get-tuple-element.59), channel_id=1, source_target_pairs={{0,1},{1,0},{2,3},{3,2},{4,5},{5,4},{6,7},{7,6},{8,9},{9,8},{10,11... | collective-permute-start | bytes 98312 | tf_op jit(solution)/shard_map/ppermute | solution.py:342
  277.2 3.3 %collective-permute-start.15 = (f32[4,512]{1,0:T(4,128)S(1)}, f32[4,512]{1,0:T(4,128)S(1)}, u32[]{:S(2)}, u32[]{:S(2)}) collective-permute-start(f32[4,512]{1,0:T(4,128)S(1)} %get-tuple-element.61), channel_id=1, source_target_pairs={{0,2},{1,3},{2,0},{3,1},{4,6},{5,7},{6,4},{7,5},{8,10},{9,11},{10,... | collective-permute-start | bytes 24584 | tf_op jit(solution)/shard_map/ppermute | solution.py:342
  277.8 4.0 %collective-permute-start.16 = (f32[4,512]{1,0:T(4,128)S(1)}, f32[4,512]{1,0:T(4,128)S(1)}, u32[]{:S(2)}, u32[]{:S(2)}) collective-permute-start(f32[4,512]{1,0:T(4,128)S(1)} %get-tuple-element.62), channel_id=1, source_target_pairs={{0,6},{1,7},{2,4},{3,5},{4,2},{5,3},{6,0},{7,1},{8,14},{9,15},{10,... | collective-permute-start | bytes 24584 | tf_op jit(solution)/shard_map/ppermute | solution.py:342
  279.6 4.3 %collective-permute-start.17 = (f32[4,512]{1,0:T(4,128)S(1)}, f32[4,512]{1,0:T(4,128)S(1)}, u32[]{:S(2)}, u32[]{:S(2)}) collective-permute-start(f32[4,512]{1,0:T(4,128)S(1)} %get-tuple-element.63), channel_id=1, source_target_pairs={{0,4},{1,5},{2,6},{3,7},{4,0},{5,1},{6,2},{7,3},{8,12},{9,13},{10,... | collective-permute-start | bytes 24584 | tf_op jit(solution)/shard_map/ppermute | solution.py:342
where the time goes:
time: 286 us; the launch traced here: 285 us
  Pallas kernels  241 us (84%)
  starting transfers between devices  35.1 us (12%)
  waiting for transfers between devices  7.51 us (3%)
    pallas_call x7, Pallas kernels, call(): pl.pallas_call(kernel, name=name, out_shape=out_shape, in_specs=in_specs,...  241 us
    ppermute x11, starting transfers between devices, swap(): return lax.ppermute(value, AXES, [(i, partner(i)) for i in range(256)])  18.4 us
    ppermute x7, starting transfers between devices, ring(): return lax.ppermute(value, AXES, [(i, partner(i)) for i in range(256)])  11 us
    ppermute x11, waiting for transfers between devices, swap(): return lax.ppermute(value, AXES, [(i, partner(i)) for i in range(256)])  7.48 us
  transfers between devices with their start and end apart: 19, of which 5 were waited for; matrix products, arithmetic and copies ran while one was open for 0% of the time, Pallas kernels for 6%

commit v1 on v0

--- a/solution.py
+++ b/solution.py
@@ -387,14 +387,14 @@
     ka = jnp.concatenate([k, by_x[0], by_x[2], by_x[1]])
     kb = swap(ka, core=1)
     ahead = 1 - 2 * (z & 1)
-    z_of = [(z + off * ahead) % 8 for off in (0, 1, -1, 2, -2, 3, -3, 4)]
+    z_of = [(z + off * ahead) % 8 for off in (0, -1, 1, -2, 2, -3, 3, 4)]
     sc = jnp.stack([me["core"], me["x"], me["y"], z] + z_of).astype(jnp.int32)
 
     half_sums = [pltpu.VMEM((PIECE, 128), jnp.float32)] * 2
     piece_rows = pltpu.VMEM((PIECE, 2 * CH), jnp.bfloat16)
     plain = [pltpu.VMEM((PIECE, CH), jnp.bfloat16)] * 2
     two = [pltpu.VMEM((2 * PIECE, 2 * CH), jnp.bfloat16)] + [pltpu.VMEM((2 * PIECE, 128), jnp.float32)] * 2
-    pieces = [own, ring(own, 0), ring(own, 1)]
+    pieces = [own, ring(own, 1), ring(own, 0)]
     kp, acc, r0 = call(
         first_kernel, "first", (sc, ka, kb, own), [SMEM, VMEM, VMEM, VMEM],
         [jax.ShapeDtypeStruct((BAND, CH), jnp.bfloat16), f32(3, 8, BAND), f32(1, 4, 4, 128)],
@@ -403,7 +403,7 @@
     parts = [r0]
     for first in (1, 3, 5):
         up, down, acc = lax.optimization_barrier((pieces[first], pieces[first + 1], acc))
-        pieces += [ring(down, 0), ring(up, 1)] if first < 5 else [ring(down, 0)]
+        pieces += [ring(down, 1), ring(up, 0)] if first < 5 else [ring(up, 0)]
         acc, got = call(
             functools.partial(more_kernel, first), f"more{first}",
             (sc, kp, acc, up, down), [SMEM] + [VMEM] * 4,

time: 286 us -> 285 us (level)
  transfers between devices with their start and end apart: 19 -> 19, of which waited for: 5 -> 6; matrix products, arithmetic and copies ran while one was open for 0% -> 0% of each run, Pallas kernels for 6% -> 6%
where the time goes in v1:
time: 285 us; the launch traced here: 284 us
  Pallas kernels  241 us (85%)
  starting transfers between devices  33.8 us (12%)
  waiting for transfers between devices  8.04 us (3%)
    pallas_call x7, Pallas kernels, call(): pl.pallas_call(kernel, name=name, out_shape=out_shape, in_specs=in_specs,...  241 us
    ppermute x11, starting transfers between devices, swap(): return lax.ppermute(value, AXES, [(i, partner(i)) for i in range(256)])  18 us
    ppermute x7, starting transfers between devices, ring(): return lax.ppermute(value, AXES, [(i, partner(i)) for i in range(256)])  11.2 us
    ppermute x11, waiting for transfers between devices, swap(): return lax.ppermute(value, AXES, [(i, partner(i)) for i in range(256)])  7.47 us
  transfers between devices with their start and end apart: 19, of which 6 were waited for; matrix products, arithmetic and copies ran while one was open for 0% of the time, Pallas kernels for 6%

profile of v1, /device:TPU:1, one launch (start us, length us, event | category | flops | bytes accessed | tf_op | source)
XLA Modules:
  0.0 284.4 jit_solution(14598479054979665371)
XLA Ops:
  0.6 2.2 collective-permute-start
  2.8 1.2 collective-permute-start.3
  4.1 1.8 collective-permute-start.4
  6.5 1.9 collective-permute-start.1
  9.1 0.9 constant_dynamic-update-slice_fusion.3
  10.1 0.9 collective-permute-done.1
  11.0 2.2 collective-permute-done.2
  13.3 2.7 collective-permute-start.6
  16.1 5.7 %collective-permute-start.7 = (bf16[512,128]{1,0:T(8,128)(2,1)S(1)}, bf16[512,128]{1,0:T(8,128)(2,1)S(1)}, u32[]{:S(2)}, u32[]{:S(2)}) collective-permute-start(bf16[512,128]{1,0:T(8,128)(2,1)S(1)} %constant_dynamic-update-slice_fusion.4.q.refs_0_), channel_id=1, source_target_pairs={{0,152},{1,153},{2,154},{3,155},{4,156},{5,157},{6,158},{7,159},{8... | collective-permute-start | bytes 393224 | tf_op jit(solution)/shard_map/ppermute | solution.py:352
  21.8 3.4 %first.1 = (bf16[4096,128]{1,0:T(8,128)(2,1)S(1)}, f32[3,8,4096]{2,1,0:T(8,128)S(1)}, f32[1,4,4,128]{3,2,1,0:T(4,128)S(1)}) custom-call(s32[12]{0:T(128)S(1)} %stack.51.sc, bf16[2048,128]{1,0:T(8,128)(2,1)S(1)} %constant_dynamic-update-slice_fusion.ka, bf16[2048,128]{1,0:T(8,128)(2,1)S(1)} %collective-permute-done.6.kb, ...), custom_call_target="tpu_custom_call" | custom-call | flops 1073741824 | bytes 2097152 | tf_op jit(solution)/shard_map/first/pallas_call | solution.py:365
  25.8 1.0 collective-permute-start.10
  27.4 4.9 %more1.1 = (f32[3,8,4096]{2,1,0:T(8,128)S(1)}, f32[2,4,4,128]{3,2,1,0:T(4,128)S(1)}) custom-call(s32[12]{0:T(128)S(1)} %stack.51.sc, bf16[4096,128]{1,0:T(8,128)(2,1)S(1)} %get-tuple-element.39.kp, f32[3,8,4096]{2,1,0:T(8,128)S(1)} %get-tuple-element.43.old, bf16[512,128]{1,0:T(8,128)(2,1)S(1)} %collective-permute-done.7.refs_0_.refs_1_, ...), custom_call_target="tpu_custom_call" | custom-call | flops 2147483648 | bytes 2097152 | tf_op jit(solution)/shard_map/more1/pallas_call | solution.py:365
  32.3 2.2 collective-permute-start.11
  34.5 4.9 %more3.1 = (f32[3,8,4096]{2,1,0:T(8,128)S(1)}, f32[2,4,4,128]{3,2,1,0:T(4,128)S(1)}) custom-call(s32[12]{0:T(128)S(1)} %stack.51.sc, bf16[4096,128]{1,0:T(8,128)(2,1)S(1)} %get-tuple-element.39.kp, f32[3,8,4096]{2,1,0:T(8,128)S(1)} %get-tuple-element.47.old, bf16[512,128]{1,0:T(8,128)(2,1)S(1)} %collective-permute-done.9.refs_0_.refs_3_, ...), custom_call_target="tpu_custom_call" | custom-call | flops 2147483648 | bytes 2097152 | tf_op jit(solution)/shard_map/more3/pallas_call | solution.py:365
  39.3 1.8 collective-permute-start.13
  41.1 4.9 %more5.1 = (f32[3,8,4096]{2,1,0:T(8,128)S(1)}, f32[2,4,4,128]{3,2,1,0:T(4,128)S(1)}) custom-call(s32[12]{0:T(128)S(1)} %stack.51.sc, bf16[4096,128]{1,0:T(8,128)(2,1)S(1)} %get-tuple-element.39.kp, f32[3,8,4096]{2,1,0:T(8,128)S(1)} %get-tuple-element.49.old, bf16[512,128]{1,0:T(8,128)(2,1)S(1)} %collective-permute-done.11.refs_0_.refs_5_, ...), custom_call_target="tpu_custom_call" | custom-call | flops 2147483648 | bytes 2097152 | tf_op jit(solution)/shard_map/more5/pallas_call | solution.py:365
  46.0 221.3 %last.1 = (f32[32,4,128]{2,1,0:T(4,128)}, f32[4,4,512]{2,1,0:T(4,128)S(1)}, f32[4,4,512]{2,1,0:T(4,128)S(1)}) custom-call(s32[12]{0:T(128)S(1)} %stack.51.sc, bf16[4096,128]{1,0:T(8,128)(2,1)S(1)} %get-tuple-element.39.kp, f32[3,8,4096]{2,1,0:T(8,128)S(1)} %get-tuple-element.52.old, bf16[512,128]{1,0:T(8,128)(2,1)S(1)} %collective-permute-done.13.q.refs_7_, ...), custom_call_target="tpu_custom_call" | custom-call | flops 1073741824 | bytes 2097152 | tf_op jit(solution)/shard_map/last/pallas_call | solution.py:365
  267.2 4.6 %all-to-all-start = ((f32[32,4,128]{2,1,0:T(4,128)}), f32[32,4,128]{2,1,0:T(4,128)S(1)}, u32[]{:S(2)}, u32[]{:S(2)}) async-start(f32[32,4,128]{2,1,0:T(4,128)} %get-tuple-element.57), calls=%async_computation | async-start | bytes 131072 | tf_op jit(solution)/shard_map/all_to_all | solution.py:424
  271.8 3.5 %collective-permute-start.14 = (f32[4,4,512]{2,1,0:T(4,128)S(1)}, f32[4,4,512]{2,1,0:T(4,128)S(1)}, u32[]{:S(2)}, u32[]{:S(2)}) collective-permute-start(f32[4,4,512]{2,1,0:T(4,128)S(1)} %get-tuple-element.59), channel_id=1, source_target_pairs={{0,1},{1,0},{2,3},{3,2},{4,5},{5,4},{6,7},{7,6},{8,9},{9,8},{10,11... | collective-permute-start | bytes 98312 | tf_op jit(solution)/shard_map/ppermute | solution.py:342
  275.3 0.9 collective-permute-done.14.b
  277.0 1.8 collective-permute-start.16
  279.7 1.3 collective-permute-done.16.k2
  281.0 2.1 collective-permute-done.17.k3
  283.2 1.2 finish.1
  (32 shorter events, 4.4 us)
Async XLA Ops:
  0.6 7.8 %collective-permute-start = (bf16[128,128]{1,0:T(8,128)(2,1)}, bf16[128,128]{1,0:T(8,128)(2,1)S(1)}, u32[]{:S(2)}, u32[]{:S(2)}) collective-permute-start(bf16[128,128]{1,0:T(8,128)(2,1)} %param.2), channel_id=1, source_target_pairs={{0,32},{1,33},{2,34},{3,35},{4,36},{5,37},{6,38},{7,39},{8,40},{9,... | collective-permute-start | bytes 98312 | tf_op jit(solution)/shard_map/ppermute | solution.py:342
  2.8 10.3 %collective-permute-start.3 = (bf16[512,128]{1,0:T(8,128)(2,1)}, bf16[512,128]{1,0:T(8,128)(2,1)S(1)}, u32[]{:S(2)}, u32[]{:S(2)}) collective-permute-start(bf16[512,128]{1,0:T(8,128)(2,1)} %param.3), channel_id=1, source_target_pairs={{0,2},{1,3},{2,0},{3,1},{4,6},{5,7},{6,4},{7,5},{8,10},{9,11},{10,... | collective-permute-start | bytes 393224 | tf_op jit(solution)/shard_map/ppermute | solution.py:342
  4.1 9.1 %collective-permute-start.4 = (bf16[512,128]{1,0:T(8,128)(2,1)}, bf16[512,128]{1,0:T(8,128)(2,1)S(1)}, u32[]{:S(2)}, u32[]{:S(2)}) collective-permute-start(bf16[512,128]{1,0:T(8,128)(2,1)} %param.3), channel_id=1, source_target_pairs={{0,6},{1,7},{2,4},{3,5},{4,2},{5,3},{6,0},{7,1},{8,14},{9,15},{10,... | collective-permute-start | bytes 393224 | tf_op jit(solution)/shard_map/ppermute | solution.py:342
  5.9 7.3 %collective-permute-start.5 = (bf16[512,128]{1,0:T(8,128)(2,1)}, bf16[512,128]{1,0:T(8,128)(2,1)S(1)}, u32[]{:S(2)}, u32[]{:S(2)}) collective-permute-start(bf16[512,128]{1,0:T(8,128)(2,1)} %param.3), channel_id=1, source_target_pairs={{0,4},{1,5},{2,6},{3,7},{4,0},{5,1},{6,2},{7,3},{8,12},{9,13},{10,... | collective-permute-start | bytes 393224 | tf_op jit(solution)/shard_map/ppermute | solution.py:342
  6.5 4.5 %collective-permute-start.1 = (bf16[128,128]{1,0:T(8,128)(2,1)}, bf16[128,128]{1,0:T(8,128)(2,1)S(1)}, u32[]{:S(2)}, u32[]{:S(2)}) collective-permute-start(bf16[128,128]{1,0:T(8,128)(2,1)} %param.2), channel_id=1, source_target_pairs={{0,96},{1,97},{2,98},{3,99},{4,100},{5,101},{6,102},{7,103},{8,104... | collective-permute-start | bytes 98312 | tf_op jit(solution)/shard_map/ppermute | solution.py:342
  8.4 4.8 %collective-permute-start.2 = (bf16[128,128]{1,0:T(8,128)(2,1)}, bf16[128,128]{1,0:T(8,128)(2,1)S(1)}, u32[]{:S(2)}, u32[]{:S(2)}) collective-permute-start(bf16[128,128]{1,0:T(8,128)(2,1)} %param.2), channel_id=1, source_target_pairs={{0,64},{1,65},{2,66},{3,67},{4,68},{5,69},{6,70},{7,71},{8,72},{9,... | collective-permute-start | bytes 98312 | tf_op jit(solution)/shard_map/ppermute | solution.py:342
  13.3 2.8 copy-start
  13.3 8.5 %collective-permute-start.6 = (bf16[2048,128]{1,0:T(8,128)(2,1)S(1)}, bf16[2048,128]{1,0:T(8,128)(2,1)S(1)}, u32[]{:S(2)}, u32[]{:S(2)}) collective-permute-start(bf16[2048,128]{1,0:T(8,128)(2,1)S(1)} %constant_dynamic-update-slice_fusion.ka), channel_id=1, source_target_pairs={{0,1},{1,0},{2,3},{3,2},{4,5},{5,4},{6,7},{7,6},{8,9},{9,8},{10,11... | collective-permute-start | bytes 1572872 | tf_op jit(solution)/shard_map/ppermute | solution.py:342
  16.1 9.2 %collective-permute-start.7 = (bf16[512,128]{1,0:T(8,128)(2,1)S(1)}, bf16[512,128]{1,0:T(8,128)(2,1)S(1)}, u32[]{:S(2)}, u32[]{:S(2)}) collective-permute-start(bf16[512,128]{1,0:T(8,128)(2,1)S(1)} %constant_dynamic-update-slice_fusion.4.q.refs_0_), channel_id=1, source_target_pairs={{0,152},{1,153},{2,154},{3,155},{4,156},{5,157},{6,158},{7,159},{8... | collective-permute-start | bytes 393224 | tf_op jit(solution)/shard_map/ppermute | solution.py:352
  21.7 4.1 %collective-permute-start.8 = (bf16[512,128]{1,0:T(8,128)(2,1)S(1)}, bf16[512,128]{1,0:T(8,128)(2,1)S(1)}, u32[]{:S(2)}, u32[]{:S(2)}) collective-permute-start(bf16[512,128]{1,0:T(8,128)(2,1)S(1)} %constant_dynamic-update-slice_fusion.4.q.refs_0_), channel_id=1, source_target_pairs={{0,128},{1,129},{2,130},{3,131},{4,132},{5,133},{6,134},{7,135},{8... | collective-permute-start | bytes 393224 | tf_op jit(solution)/shard_map/ppermute | solution.py:352
  25.8 6.4 %collective-permute-start.10 = (bf16[512,128]{1,0:T(8,128)(2,1)S(1)}, bf16[512,128]{1,0:T(8,128)(2,1)S(1)}, u32[]{:S(2)}, u32[]{:S(2)}) collective-permute-start(bf16[512,128]{1,0:T(8,128)(2,1)S(1)} %collective-permute-done.7.refs_0_.refs_1_), channel_id=1, source_target_pairs={{0,128},{1,129},{2,130},{3,131},{4,132},{5,133},{6,134},{7,135},{8... | collective-permute-start | bytes 393224 | tf_op jit(solution)/shard_map/ppermute | solution.py:352
  26.8 5.4 %collective-permute-start.9 = (bf16[512,128]{1,0:T(8,128)(2,1)S(1)}, bf16[512,128]{1,0:T(8,128)(2,1)S(1)}, u32[]{:S(2)}, u32[]{:S(2)}) collective-permute-start(bf16[512,128]{1,0:T(8,128)(2,1)S(1)} %collective-permute-done.8.refs_1_.refs_2_), channel_id=1, source_target_pairs={{0,152},{1,153},{2,154},{3,155},{4,156},{5,157},{6,158},{7,159},{8... | collective-permute-start | bytes 393224 | tf_op jit(solution)/shard_map/ppermute | solution.py:352
  32.3 7.1 %collective-permute-start.11 = (bf16[512,128]{1,0:T(8,128)(2,1)S(1)}, bf16[512,128]{1,0:T(8,128)(2,1)S(1)}, u32[]{:S(2)}, u32[]{:S(2)}) collective-permute-start(bf16[512,128]{1,0:T(8,128)(2,1)S(1)} %collective-permute-done.10.refs_1_.refs_4_), channel_id=1, source_target_pairs={{0,152},{1,153},{2,154},{3,155},{4,156},{5,157},{6,158},{7,159},{8... | collective-permute-start | bytes 393224 | tf_op jit(solution)/shard_map/ppermute | solution.py:352
  34.4 4.9 %collective-permute-start.12 = (bf16[512,128]{1,0:T(8,128)(2,1)S(1)}, bf16[512,128]{1,0:T(8,128)(2,1)S(1)}, u32[]{:S(2)}, u32[]{:S(2)}) collective-permute-start(bf16[512,128]{1,0:T(8,128)(2,1)S(1)} %collective-permute-done.9.refs_0_.refs_3_), channel_id=1, source_target_pairs={{0,128},{1,129},{2,130},{3,131},{4,132},{5,133},{6,134},{7,135},{8... | collective-permute-start | bytes 393224 | tf_op jit(solution)/shard_map/ppermute | solution.py:352
  39.3 6.6 %collective-permute-start.13 = (bf16[512,128]{1,0:T(8,128)(2,1)S(1)}, bf16[512,128]{1,0:T(8,128)(2,1)S(1)}, u32[]{:S(2)}, u32[]{:S(2)}) collective-permute-start(bf16[512,128]{1,0:T(8,128)(2,1)S(1)} %collective-permute-done.11.refs_0_.refs_5_), channel_id=1, source_target_pairs={{0,128},{1,129},{2,130},{3,131},{4,132},{5,133},{6,134},{7,135},{8... | collective-permute-start | bytes 393224 | tf_op jit(solution)/shard_map/ppermute | solution.py:352
  267.2 15.9 %all-to-all-start = ((f32[32,4,128]{2,1,0:T(4,128)}), f32[32,4,128]{2,1,0:T(4,128)S(1)}, u32[]{:S(2)}, u32[]{:S(2)}) async-start(f32[32,4,128]{2,1,0:T(4,128)} %get-tuple-element.57), calls=%async_computation | async-start | bytes 131072 | tf_op jit(solution)/shard_map/all_to_all | solution.py:424
  271.8 4.4 %collective-permute-start.14 = (f32[4,4,512]{2,1,0:T(4,128)S(1)}, f32[4,4,512]{2,1,0:T(4,128)S(1)}, u32[]{:S(2)}, u32[]{:S(2)}) collective-permute-start(f32[4,4,512]{2,1,0:T(4,128)S(1)} %get-tuple-element.59), channel_id=1, source_target_pairs={{0,1},{1,0},{2,3},{3,2},{4,5},{5,4},{6,7},{7,6},{8,9},{9,8},{10,11... | collective-permute-start | bytes 98312 | tf_op jit(solution)/shard_map/ppermute | solution.py:342
  276.4 3.3 %collective-permute-start.15 = (f32[4,512]{1,0:T(4,128)S(1)}, f32[4,512]{1,0:T(4,128)S(1)}, u32[]{:S(2)}, u32[]{:S(2)}) collective-permute-start(f32[4,512]{1,0:T(4,128)S(1)} %get-tuple-element.61), channel_id=1, source_target_pairs={{0,2},{1,3},{2,0},{3,1},{4,6},{5,7},{6,4},{7,5},{8,10},{9,11},{10,... | collective-permute-start | bytes 24584 | tf_op jit(solution)/shard_map/ppermute | solution.py:342
  277.0 4.0 %collective-permute-start.16 = (f32[4,512]{1,0:T(4,128)S(1)}, f32[4,512]{1,0:T(4,128)S(1)}, u32[]{:S(2)}, u32[]{:S(2)}) collective-permute-start(f32[4,512]{1,0:T(4,128)S(1)} %get-tuple-element.62), channel_id=1, source_target_pairs={{0,6},{1,7},{2,4},{3,5},{4,2},{5,3},{6,0},{7,1},{8,14},{9,15},{10,... | collective-permute-start | bytes 24584 | tf_op jit(solution)/shard_map/ppermute | solution.py:342
  278.9 4.3 %collective-permute-start.17 = (f32[4,512]{1,0:T(4,128)S(1)}, f32[4,512]{1,0:T(4,128)S(1)}, u32[]{:S(2)}, u32[]{:S(2)}) collective-permute-start(f32[4,512]{1,0:T(4,128)S(1)} %get-tuple-element.63), channel_id=1, source_target_pairs={{0,4},{1,5},{2,6},{3,7},{4,0},{5,1},{6,2},{7,3},{8,12},{9,13},{10,... | collective-permute-start | bytes 24584 | tf_op jit(solution)/shard_map/ppermute | solution.py:342
